TPU v7x, 32 devices: a whole 2x2x4 slice. The times are simulated.
32 devices in a mesh: batch: 8 (over z, x), tm: 4 (over y, core).
Axes of the slice: x: 2, y: 2, z: 4, core: 2. Of those that a mesh axis runs over, the one named last changes fastest.
Arguments:
- input_small: bfloat16 [16, 4, 7, 7, 512], P('batch', 'tm'), may hold values from -15 to 15
- input_large: bfloat16 [16, 4, 10, 10, 512], P('batch', 'tm'), may hold values from -15 to 15
- spatial_one: bfloat16 [9, 512, 1152], P(None, ('batch', 'tm')), may hold values from -0.09375 to 0.09375
- temporal_one: bfloat16 [3, 1152, 512], P(None, None, ('batch', 'tm')), may hold values from -0.109375 to 0.109375
- spatial_two: bfloat16 [9, 512, 1152], P(None, ('batch', 'tm')), may hold values from -0.09375 to 0.09375
- temporal_two: bfloat16 [3, 1152, 512], P(None, None, ('batch', 'tm')), may hold values from -0.109375 to 0.109375
- mid_gain: float32 [2, 1152], replicated, may hold values from 0.1 to 1.9
- mid_shift: float32 [2, 1152], replicated, may hold values from -3 to 3
- out_gain: float32 [2, 512], replicated, may hold values from 0.1 to 1.9
- out_shift: float32 [2, 512], replicated, may hold values from -3 to 3
- cotangent_small: bfloat16 [16, 4, 7, 7, 512], P('batch', 'tm'), may hold values from -6 to 6
- cotangent_large: bfloat16 [16, 4, 10, 10, 512], P('batch', 'tm'), may hold values from -6 to 6
Outputs:
- output_small: bfloat16 [16, 4, 7, 7, 512], P('batch', 'tm')
- output_large: bfloat16 [16, 4, 10, 10, 512], P('batch', 'tm')
- grad_small: float32 [16, 4, 7, 7, 512], P('batch', 'tm')
- grad_large: float32 [16, 4, 10, 10, 512], P('batch', 'tm')
- grad_spatial_one: float32 [9, 512, 1152], P(None, ('batch', 'tm'))
- grad_temporal_one: float32 [3, 1152, 512], P(None, None, ('batch', 'tm'))
- grad_spatial_two: float32 [9, 512, 1152], P(None, ('batch', 'tm'))
- grad_temporal_two: float32 [3, 1152, 512], P(None, None, ('batch', 'tm'))
- grad_mid_gain: float32 [2, 1152], replicated
- grad_mid_shift: float32 [2, 1152], replicated
- grad_out_gain: float32 [2, 512], replicated
- grad_out_shift: float32 [2, 512], replicated
All inputs are finite; a program needn't handle non-finite values.
Results may differ from a plain program's by a relative error of at most 0.025.
Values may be sent and summed in bfloat16 or wider, within the bound.
No kernel may reach another device: no remote copies, remote signals or barrier semaphores. Data moves between devices by JAX's collectives and lax.ppermute only.
A program may use at most 320 MiB of HBM per device.

v0:
```python
import jax
import jax.numpy as jnp
from jax import lax
from jax.sharding import PartitionSpec as P

EPS = 1e-05


def cut_along(value, dim, length):
    before, after = (value.shape[:dim], value.shape[dim + 1 :])
    return jnp.moveaxis(value.reshape(*before, length, -1, *after), dim, 0)


def sent_and_summed(value, axis, dim):
    length = lax.axis_size(axis)
    pieces = lax.all_to_all(cut_along(value, dim, length), axis, 0, 0, tiled=True)
    return jnp.sum(pieces.astype(jnp.float32), axis=0)


def side_by_side(arrays, axis, dim, along):
    both = jnp.concatenate(arrays, axis=along)
    result, at, done = (sent_and_summed(both, axis, dim), 0, [])
    for a in arrays:
        done.append(lax.slice_in_dim(result, at, at + a.shape[along], axis=along))
        at += a.shape[along]
    return tuple(done)


def silu_slope(value):
    sigma = jax.nn.sigmoid(value)
    return sigma * (1.0 + value * (1.0 - sigma))


def contract_rows(left, right):
    return lax.dot_general(
        left, right, (((0,), (0,)), ((), ())), preferred_element_type=jnp.float32
    )


def contract_cols(left, right):
    return lax.dot_general(
        left, right, (((1,), (1,)), ((), ())), preferred_element_type=jnp.float32
    )


def space_patches(value):
    count, frames, height, width, chans = value.shape
    padded = jnp.pad(value, ((0, 0), (0, 0), (1, 1), (1, 1), (0, 0)))
    pieces = [padded[:, :, i : i + height, j : j + width] for i in range(3) for j in range(3)]
    return jnp.stack(pieces, axis=4).reshape(count * frames * height * width, 9 * chans)


def space_spread(grad_rows, shape):
    count, frames, height, width, chans = shape
    blocks = grad_rows.reshape(count, frames, height, width, 9, chans)
    padded = jnp.zeros((count, frames, height + 2, width + 2, chans), jnp.float32)
    for i in range(3):
        for j in range(3):
            padded = padded.at[:, :, i : i + height, j : j + width].add(
                blocks[:, :, :, :, 3 * i + j]
            )
    return padded[:, :, 1 : height + 1, 1 : width + 1]


def time_patches(value):
    count, frames, places, chans = value.shape
    padded = jnp.pad(value, ((0, 0), (1, 1), (0, 0), (0, 0)))
    pieces = [padded[:, k : k + frames] for k in range(3)]
    return jnp.stack(pieces, axis=3).reshape(count * frames * places, 3 * chans)


def time_spread(grad_rows, shape):
    count, frames, places, chans = shape
    blocks = grad_rows.reshape(count, frames, places, 3, chans)
    padded = jnp.zeros((count, frames + 2, places, chans), jnp.float32)
    for k in range(3):
        padded = padded.at[:, k : k + frames].add(blocks[:, :, :, k])
    return padded[:, 1 : frames + 1]


def spatial_forward(value, kernel):
    result = jnp.dot(
        space_patches(value),
        kernel.reshape(-1, kernel.shape[2]),
        preferred_element_type=jnp.float32,
    )
    return result.reshape(value.shape[:4] + (kernel.shape[2],))


def temporal_forward(value, kernel):
    result = jnp.dot(
        time_patches(value), kernel.reshape(-1, kernel.shape[2]), preferred_element_type=jnp.float32
    )
    return result.reshape(value.shape[:3] + (kernel.shape[2],))


def spatial_backward(inputs, grads, kernel):
    flat_kernel = kernel.reshape(-1, kernel.shape[2])
    kernel_grad = jnp.zeros(flat_kernel.shape, jnp.float32)
    input_grads = []
    for value, grad in zip(inputs, grads):
        grad_rows = grad.reshape(-1, grad.shape[-1])
        kernel_grad = kernel_grad + contract_rows(space_patches(value), grad_rows)
        input_grads.append(space_spread(contract_cols(grad_rows, flat_kernel), value.shape))
    return (kernel_grad.reshape(kernel.shape), input_grads)


def temporal_backward(inputs, grads, kernel):
    flat_kernel = kernel.reshape(-1, kernel.shape[2])
    kernel_grad = jnp.zeros(flat_kernel.shape, jnp.float32)
    input_grads = []
    for value, grad in zip(inputs, grads):
        grad_rows = grad.reshape(-1, grad.shape[-1])
        kernel_grad = kernel_grad + contract_rows(time_patches(value), grad_rows)
        input_grads.append(
            time_spread(contract_cols(grad_rows, flat_kernel), value.shape).astype(jnp.bfloat16)
        )
    return (kernel_grad.reshape(kernel.shape), input_grads)


def spread_out(vector, place):
    whole, offset = place
    return lax.dynamic_update_slice(jnp.zeros((whole,), jnp.float32), vector, (offset,))


def own_slice(vector, place, share):
    return lax.dynamic_slice_in_dim(vector, place[1], share)


def moments(parts, place):
    totals = sum((jnp.sum(p, axis=(0, 1, 2, 3)) for p in parts))
    squares = sum((jnp.sum(p * p, axis=(0, 1, 2, 3)) for p in parts))
    share = totals.shape[0]
    local_rows = sum((p.size // p.shape[-1] for p in parts))
    if place is not None:
        totals = spread_out(totals, place)
        squares = spread_out(squares, place)
    totals, squares = lax.psum((totals, squares), ("batch", "tm"))
    if place is not None:
        totals = own_slice(totals, place, share)
        squares = own_slice(squares, place, share)
        counted = float(local_rows * lax.axis_size("batch"))
    else:
        counted = float(local_rows * lax.axis_size("batch") * lax.axis_size("tm"))
    average = totals / counted
    spread = squares / counted - average * average
    return (average, lax.rsqrt(spread + EPS), counted)


def normalize(parts, stats, gain, shift):
    average, inverse, counted = stats
    scaled = [(p - average) * inverse for p in parts]
    return (scaled, [gain * s + shift for s in scaled])


def norm_back(grads, scaled, gain, stats, place):
    average, inverse, counted = stats
    gain_local = sum((jnp.sum(g * s, axis=(0, 1, 2, 3)) for g, s in zip(grads, scaled)))
    shift_local = sum((jnp.sum(g, axis=(0, 1, 2, 3)) for g in grads))
    share = gain_local.shape[0]
    if place is not None:
        gain_local = spread_out(gain_local, place)
        shift_local = spread_out(shift_local, place)
    gain_full, shift_full = lax.psum((gain_local, shift_local), ("batch", "tm"))
    gain_grad, shift_grad = (gain_full, shift_full)
    if place is not None:
        gain_grad = own_slice(gain_full, place, share)
        shift_grad = own_slice(shift_full, place, share)
    back = [
        gain * inverse * (g - (shift_grad + s * gain_grad) / counted) for g, s in zip(grads, scaled)
    ]
    return (back, gain_full, shift_full)


def whole_frames(parts):
    moved = (
        lax.all_gather(parts[0], "tm", axis=1, tiled=True),
        lax.all_gather(parts[1], "tm", axis=1, tiled=True),
    )
    return [moved[0], moved[1]]


def frame_sum(parts):
    moved = (
        lax.psum_scatter(
            parts[0].astype(jnp.bfloat16), "tm", scatter_dimension=1, tiled=True
        ).astype(jnp.float32),
        lax.psum_scatter(
            parts[1].astype(jnp.bfloat16), "tm", scatter_dimension=1, tiled=True
        ).astype(jnp.float32),
    )
    return [moved[0], moved[1]]


def split_kernels(shards):
    first_s, first_t, second_s, second_t = shards
    moved = (
        lax.all_to_all(first_s, "tm", split_axis=2, concat_axis=1, tiled=True),
        lax.all_to_all(jnp.swapaxes(first_t, 1, 2), "tm", split_axis=2, concat_axis=1, tiled=True),
        lax.all_to_all(second_s, "tm", split_axis=2, concat_axis=1, tiled=True),
        lax.all_to_all(jnp.swapaxes(second_t, 1, 2), "tm", split_axis=2, concat_axis=1, tiled=True),
    )
    whole = (
        lax.all_gather(moved[0], "batch", axis=1, tiled=True),
        lax.all_gather(moved[1], "batch", axis=1, tiled=True),
        lax.all_gather(moved[2], "batch", axis=1, tiled=True),
        lax.all_gather(moved[3], "batch", axis=1, tiled=True),
    )
    return (whole[0], jnp.swapaxes(whole[1], 1, 2), whole[2], jnp.swapaxes(whole[3], 1, 2))


def temporal_clips(value, kernel):
    count, frames, height, width, chans = value.shape
    result = temporal_forward(value.reshape(count, frames, height * width, chans), kernel)
    return result.reshape(count, frames, height, width, kernel.shape[2])


def temporal_clips_back(inputs, grads, kernel):
    flat_inputs = [
        v.reshape(v.shape[0], v.shape[1], v.shape[2] * v.shape[3], v.shape[4]) for v in inputs
    ]
    flat_grads = [
        g.reshape(g.shape[0], g.shape[1], g.shape[2] * g.shape[3], g.shape[4]) for g in grads
    ]
    kernel_grad, input_grads = temporal_backward(flat_inputs, flat_grads, kernel)
    return (kernel_grad, [d.reshape(v.shape) for d, v in zip(input_grads, inputs)])


def finish(outputs, grad_total, kernel_grads, norm_grads):
    grad_sa, grad_ta, grad_sb, grad_tb = kernel_grads
    gain_one, shift_one, gain_two, shift_two, gain_three, shift_three, gain_four, shift_four = (
        norm_grads
    )
    return (
        outputs[0],
        outputs[1],
        grad_total[0],
        grad_total[1],
        grad_sa,
        grad_ta,
        grad_sb,
        grad_tb,
        jnp.stack([gain_one, gain_three]),
        jnp.stack([shift_one, shift_three]),
        jnp.stack([gain_two, gain_four]),
        jnp.stack([shift_two, shift_four]),
    )


def channel_layout(inputs, shards, mid_gain, mid_shift, out_gain, out_shift, cotangents):
    kernel_sa, kernel_ta, kernel_sb, kernel_tb = split_kernels(shards)
    share = kernel_sa.shape[2]
    place = (share * lax.axis_size("tm"), lax.axis_index("tm") * share)
    gain_a = own_slice(mid_gain[0], place, share)
    shift_a = own_slice(mid_shift[0], place, share)
    gain_b = own_slice(mid_gain[1], place, share)
    shift_b = own_slice(mid_shift[1], place, share)
    full_inputs = whole_frames(inputs)
    first = [spatial_forward(v, kernel_sa) for v in full_inputs]
    stats_one = moments(first, place)
    scaled_one, pre_one = normalize(first, stats_one, gain_a, shift_a)
    act_one = [jax.nn.silu(h).astype(jnp.bfloat16) for h in pre_one]
    time_one = frame_sum([temporal_clips(v, kernel_ta) for v in act_one])
    time_one = [v.astype(jnp.bfloat16).astype(jnp.float32) for v in time_one]
    stats_two = moments(time_one, None)
    scaled_two, pre_two = normalize(time_one, stats_two, out_gain[0], out_shift[0])
    middle = [jax.nn.silu(h).astype(jnp.bfloat16) for h in pre_two]
    full_middle = whole_frames(middle)
    second = [spatial_forward(v, kernel_sb) for v in full_middle]
    stats_three = moments(second, place)
    scaled_three, pre_three = normalize(second, stats_three, gain_b, shift_b)
    act_two = [jax.nn.silu(h).astype(jnp.bfloat16) for h in pre_three]
    time_two = frame_sum([temporal_clips(v, kernel_tb) for v in act_two])
    time_two = [v.astype(jnp.bfloat16).astype(jnp.float32) for v in time_two]
    stats_four = moments(time_two, None)
    scaled_four, branch = normalize(time_two, stats_four, out_gain[1], out_shift[1])
    pre_out = [v.astype(jnp.float32) + d for v, d in zip(inputs, branch)]
    outputs = [jax.nn.silu(p).astype(jnp.bfloat16) for p in pre_out]
    grad_pre = [c.astype(jnp.float32) * silu_slope(p) for c, p in zip(cotangents, pre_out)]
    back_four, gain_four, shift_four = norm_back(
        grad_pre, scaled_four, out_gain[1], stats_four, None
    )
    grad_time_two = whole_frames([g.astype(jnp.bfloat16) for g in back_four])
    grad_tb, grad_act_two = temporal_clips_back(act_two, grad_time_two, kernel_tb)
    upstream = [g.astype(jnp.float32) * silu_slope(h) for g, h in zip(grad_act_two, pre_three)]
    back_three, gain_three, shift_three = norm_back(
        upstream, scaled_three, gain_b, stats_three, place
    )
    grad_second = [g.astype(jnp.bfloat16) for g in back_three]
    grad_sb, partial_middle = spatial_backward(full_middle, grad_second, kernel_sb)
    grad_middle = frame_sum(partial_middle)
    upstream = [g * silu_slope(h) for g, h in zip(grad_middle, pre_two)]
    back_two, gain_two, shift_two = norm_back(upstream, scaled_two, out_gain[0], stats_two, None)
    grad_time_one = whole_frames([g.astype(jnp.bfloat16) for g in back_two])
    grad_ta, grad_act_one = temporal_clips_back(act_one, grad_time_one, kernel_ta)
    upstream = [g.astype(jnp.float32) * silu_slope(h) for g, h in zip(grad_act_one, pre_one)]
    back_one, gain_one, shift_one = norm_back(upstream, scaled_one, gain_a, stats_one, place)
    grad_first = [g.astype(jnp.bfloat16) for g in back_one]
    grad_sa, partial_inputs = spatial_backward(full_inputs, grad_first, kernel_sa)
    grad_inputs = frame_sum(partial_inputs)
    summed = side_by_side(
        (
            grad_sa.astype(jnp.bfloat16),
            jnp.swapaxes(grad_ta, 1, 2).astype(jnp.bfloat16),
            grad_sb.astype(jnp.bfloat16),
            jnp.swapaxes(grad_tb, 1, 2).astype(jnp.bfloat16),
        ),
        "batch",
        1,
        0,
    )
    owned = (
        lax.all_to_all(
            summed[0].astype(jnp.bfloat16), "tm", split_axis=1, concat_axis=2, tiled=True
        ).astype(jnp.float32),
        lax.all_to_all(
            summed[1].astype(jnp.bfloat16), "tm", split_axis=1, concat_axis=2, tiled=True
        ).astype(jnp.float32),
        lax.all_to_all(
            summed[2].astype(jnp.bfloat16), "tm", split_axis=1, concat_axis=2, tiled=True
        ).astype(jnp.float32),
        lax.all_to_all(
            summed[3].astype(jnp.bfloat16), "tm", split_axis=1, concat_axis=2, tiled=True
        ).astype(jnp.float32),
    )
    grad_total = [g + d for g, d in zip(grad_inputs, grad_pre)]
    return finish(
        outputs,
        grad_total,
        (owned[0], jnp.swapaxes(owned[1], 1, 2), owned[2], jnp.swapaxes(owned[3], 1, 2)),
        (gain_one, shift_one, gain_two, shift_two, gain_three, shift_three, gain_four, shift_four),
    )


def body(
    input_small,
    input_large,
    spatial_one,
    temporal_one,
    spatial_two,
    temporal_two,
    mid_gain,
    mid_shift,
    out_gain,
    out_shift,
    cotangent_small,
    cotangent_large,
):
    shards = (spatial_one, temporal_one, spatial_two, temporal_two)
    inputs = [input_small, input_large]
    cotangents = [cotangent_small, cotangent_large]
    return channel_layout(inputs, shards, mid_gain, mid_shift, out_gain, out_shift, cotangents)


def solution(mesh):
    return jax.shard_map(
        body,
        mesh=mesh,
        in_specs=(
            P("batch", "tm", None, None, None),
            P("batch", "tm", None, None, None),
            P(None, ("batch", "tm"), None),
            P(None, None, ("batch", "tm")),
            P(None, ("batch", "tm"), None),
            P(None, None, ("batch", "tm")),
            P(),
            P(),
            P(),
            P(),
            P("batch", "tm", None, None, None),
            P("batch", "tm", None, None, None),
        ),
        out_specs=(
            P("batch", "tm", None, None, None),
            P("batch", "tm", None, None, None),
            P("batch", "tm", None, None, None),
            P("batch", "tm", None, None, None),
            P(None, ("batch", "tm"), None),
            P(None, None, ("batch", "tm")),
            P(None, ("batch", "tm"), None),
            P(None, None, ("batch", "tm")),
            P(),
            P(),
            P(),
            P(),
        ),
        check_vma=False,
    )
```

profile of v0, /device:TPU:13, one launch (start us, length us, event | category | flops | bytes accessed | tf_op | source)
XLA Modules:
  0.0 1516.1 jit_solution(13146165891305335550)
XLA Ops:
  80.9 34.5 %all_gather.39 = bf16[3,512,288]{2,1,0:T(8,128)(2,1)S(1)} all-gather(bf16[3,64,288]{2,1,0:T(8,128)(2,1)S(1)} %bitcast.728), channel_id=1, replica_groups=mesh['batch'=8,'tm'=4] {'batch'}, dimensions={1}, use_global_device_ids=true | all-gather | bytes 995328 | tf_op jit(solution)/shard_map/all_gather | solution.py:205
  135.1 41.5 %all-reduce.31 = (f32[1152]{0:T(1024)S(1)}, f32[1152]{0:T(1024)S(1)}) all-reduce(f32[1152]{0:T(1024)S(1)} %add_dynamic-update-slice_fusion.6, f32[1152]{0:T(1024)S(1)} %add_dynamic-update-slice_fusion.7), channel_id=1, replica_groups=mesh['batch'=8,'tm'=4] {'batch','tm'}, use_global_device_ids=true, to_apply=%region_5.6 | all-reduce | flops 2304 | bytes 18432 | tf_op jit(solution)/shard_map/psum | solution.py:138
  242.9 30.6 %all_gather.43 = bf16[3,512,288]{2,1,0:T(8,128)(2,1)S(1)} all-gather(bf16[3,64,288]{2,1,0:T(8,128)(2,1)S(1)} %bitcast.729), channel_id=1, replica_groups=mesh['batch'=8,'tm'=4] {'batch'}, dimensions={1}, use_global_device_ids=true | all-gather | bytes 995328 | tf_op jit(solution)/shard_map/all_gather | solution.py:207
  278.5 48.4 %all-reduce.30 = (f32[512]{0:T(512)S(1)}, f32[512]{0:T(512)S(1)}) all-reduce(f32[512]{0:T(512)S(1)} %add.730, f32[512]{0:T(512)S(1)} %add.729), channel_id=1, replica_groups=mesh['batch'=8,'tm'=4] {'batch','tm'}, use_global_device_ids=true, to_apply=%region_13.14 | all-reduce | flops 1024 | bytes 8192 | tf_op jit(solution)/shard_map/psum | solution.py:138
  367.9 38.7 %all-reduce.29 = (f32[1152]{0:T(1024)S(1)}, f32[1152]{0:T(1024)S(1)}) all-reduce(f32[1152]{0:T(1024)S(1)} %add_dynamic-update-slice_fusion.4, f32[1152]{0:T(1024)S(1)} %add_dynamic-update-slice_fusion.5), channel_id=1, replica_groups=mesh['batch'=8,'tm'=4] {'batch','tm'}, use_global_device_ids=true, to_apply=%region_19.20 | all-reduce | flops 2304 | bytes 18432 | tf_op jit(solution)/shard_map/psum | solution.py:138
  455.8 16.7 %copy.731 = bf16[100,8,9,512]{3,1,2,0:T(8,128)(2,1)} copy(bf16[100,8,9,512]{3,2,1,0:T(8,128)(2,1)} %bitcast.677) | data formatting | bytes 14745600
  522.0 16.5 %copy.733 = bf16[100,8,9,512]{3,1,2,0:T(8,128)(2,1)} copy(bf16[100,8,9,512]{3,2,1,0:T(8,128)(2,1)} %bitcast.676) | data formatting | bytes 14745600
  546.9 41.3 %all-reduce.28 = (f32[512]{0:T(512)S(1)}, f32[512]{0:T(512)S(1)}) all-reduce(f32[512]{0:T(512)S(1)} %add.750, f32[512]{0:T(512)S(1)} %add.749), channel_id=1, replica_groups=mesh['batch'=8,'tm'=4] {'batch','tm'}, use_global_device_ids=true, to_apply=%region_27.28 | all-reduce | flops 1024 | bytes 8192 | tf_op jit(solution)/shard_map/psum | solution.py:138
  591.3 39.1 %all-reduce.27 = (f32[512]{0:T(512)S(1)}, f32[512]{0:T(512)S(1)}) all-reduce(f32[512]{0:T(512)S(1)} %add.765, f32[512]{0:T(512)S(1)} %add.763), channel_id=1, replica_groups=mesh['batch'=8,'tm'=4] {'batch','tm'}, use_global_device_ids=true, to_apply=%region_33.34 | all-reduce | flops 1024 | bytes 8192 | tf_op jit(solution)/shard_map/psum | solution.py:164
  667.1 39.9 %all-reduce.26 = (f32[1152]{0:T(1024)S(1)}, f32[1152]{0:T(1024)S(1)}) all-reduce(f32[1152]{0:T(1024)S(1)} %add_dynamic-update-slice_fusion.2, f32[1152]{0:T(1024)S(1)} %add_dynamic-update-slice_fusion.3), channel_id=1, replica_groups=mesh['batch'=8,'tm'=4] {'batch','tm'}, use_global_device_ids=true, to_apply=%region_39.40 | all-reduce | flops 2304 | bytes 18432 | tf_op jit(solution)/shard_map/psum | solution.py:164
  762.7 13.5 fusion.10
  783.7 19.0 %scatter-add.186 = f32[2,4,12,12,512]{4,3,2,1,0:T(8,128)S(1)} dynamic-update-slice(f32[2,4,12,12,512]{4,3,2,1,0:T(8,128)S(1)} %scatter-add.185, f32[2,4,10,10,512]{4,3,2,1,0:T(8,128)} %fusion.33, s32[]{:T(128)} %constant.1137.clone.1, s32[]{:T(128)} %constant.1137.clone.1, s32[]{:T(128)} %bitcast.134, s32[]{:T(128)} %bitcast.135, s32[]{:T(128)} %constant.1137.clone.1) | dynamic-update-slice | bytes 3276804 | tf_op jit(solution)/shard_map/scatter-add | solution.py:59
  808.5 19.1 %scatter-add.189 = f32[2,4,12,12,512]{4,3,2,1,0:T(8,128)S(1)} dynamic-update-slice(f32[2,4,12,12,512]{4,3,2,1,0:T(8,128)S(1)} %scatter-add.186, f32[2,4,10,10,512]{4,3,2,1,0:T(8,128)} %add_select_fusion.1, s32[]{:T(128)} %constant.1137.clone.1, s32[]{:T(128)} %constant.1137.clone.1, s32[]{:T(128)} %bitcast.137, s32[]{:T(128)} %bitcast.138, s32[]{:T(128)} %constant.1137.clone.1) | dynamic-update-slice | bytes 3276804 | tf_op jit(solution)/shard_map/scatter-add | solution.py:59
  831.4 17.6 %scatter-add.190 = f32[2,4,12,12,512]{4,3,2,1,0:T(8,128)S(1)} dynamic-update-slice(f32[2,4,12,12,512]{4,3,2,1,0:T(8,128)S(1)} %scatter-add.189, f32[2,4,10,10,512]{4,3,2,1,0:T(8,128)} %fusion.32, s32[]{:T(128)} %constant.1137.clone.1, s32[]{:T(128)} %constant.1137.clone.1, s32[]{:T(128)} %constant.1146.clone.1, s32[]{:T(128)} %constant.1137.clone.1, s32[]{:T(128)} %constant.1137.clone.1) | dynamic-update-slice | bytes 3276804 | tf_op jit(solution)/shard_map/scatter-add | solution.py:59
  853.1 17.6 %scatter-add.191 = f32[2,4,12,12,512]{4,3,2,1,0:T(8,128)S(1)} dynamic-update-slice(f32[2,4,12,12,512]{4,3,2,1,0:T(8,128)S(1)} %scatter-add.190, f32[2,4,10,10,512]{4,3,2,1,0:T(8,128)} %fusion.31, s32[]{:T(128)} %constant.1137.clone.1, s32[]{:T(128)} %constant.1137.clone.1, s32[]{:T(128)} %constant.1146.clone.1, s32[]{:T(128)} %constant.1146.clone.1, s32[]{:T(128)} %constant.1137.clone.1) | dynamic-update-slice | bytes 3276804 | tf_op jit(solution)/shard_map/scatter-add | solution.py:59
  874.7 17.6 %scatter-add.194 = f32[2,4,12,12,512]{4,3,2,1,0:T(8,128)S(1)} dynamic-update-slice(f32[2,4,12,12,512]{4,3,2,1,0:T(8,128)S(1)} %scatter-add.191, f32[2,4,10,10,512]{4,3,2,1,0:T(8,128)} %fusion.30, s32[]{:T(128)} %constant.1137.clone.1, s32[]{:T(128)} %constant.1137.clone.1, s32[]{:T(128)} %constant.1146.clone.1, s32[]{:T(128)} %constant.1147.clone.1, s32[]{:T(128)} %constant.1137.clone.1) | dynamic-update-slice | bytes 3276804 | tf_op jit(solution)/shard_map/scatter-add | solution.py:59
  896.2 17.5 %scatter-add.195 = f32[2,4,12,12,512]{4,3,2,1,0:T(8,128)S(1)} dynamic-update-slice(f32[2,4,12,12,512]{4,3,2,1,0:T(8,128)S(1)} %scatter-add.194, f32[2,4,10,10,512]{4,3,2,1,0:T(8,128)} %fusion.29, s32[]{:T(128)} %constant.1137.clone.1, s32[]{:T(128)} %constant.1137.clone.1, s32[]{:T(128)} %constant.1147.clone.1, s32[]{:T(128)} %constant.1137.clone.1, s32[]{:T(128)} %constant.1137.clone.1) | dynamic-update-slice | bytes 3276804 | tf_op jit(solution)/shard_map/scatter-add | solution.py:59
  917.7 17.5 %scatter-add.196 = f32[2,4,12,12,512]{4,3,2,1,0:T(8,128)S(1)} dynamic-update-slice(f32[2,4,12,12,512]{4,3,2,1,0:T(8,128)S(1)} %scatter-add.195, f32[2,4,10,10,512]{4,3,2,1,0:T(8,128)} %fusion.28, s32[]{:T(128)} %constant.1137.clone.1, s32[]{:T(128)} %constant.1137.clone.1, s32[]{:T(128)} %constant.1147.clone.1, s32[]{:T(128)} %constant.1146.clone.1, s32[]{:T(128)} %constant.1137.clone.1) | dynamic-update-slice | bytes 3276804 | tf_op jit(solution)/shard_map/scatter-add | solution.py:59
  939.2 17.7 %scatter-add.199 = f32[2,4,12,12,512]{4,3,2,1,0:T(8,128)S(1)} dynamic-update-slice(f32[2,4,12,12,512]{4,3,2,1,0:T(8,128)S(1)} %scatter-add.196, f32[2,4,10,10,512]{4,3,2,1,0:T(8,128)} %fusion.27, s32[]{:T(128)} %constant.1137.clone.1, s32[]{:T(128)} %constant.1137.clone.1, s32[]{:T(128)} %constant.1147.clone.1, s32[]{:T(128)} %constant.1147.clone.1, s32[]{:T(128)} %constant.1137.clone.1) | dynamic-update-slice | bytes 3276804 | tf_op jit(solution)/shard_map/scatter-add | solution.py:59
  984.4 22.7 %all-reduce.43.cloned.1.call-done = (bf16[2,4,7,7,512]{4,0,3,2,1:T(2,128)(2,1)}, bf16[2,4,10,10,512]{4,0,3,2,1:T(2,128)(2,1)}) async-done(((bf16[2,4,7,7,512]{4,0,3,2,1:T(2,128)(2,1)}, bf16[2,4,10,10,512]{4,0,3,2,1:T(2,128)(2,1)}), (bf16[2,4,7,7,512]{4,0,3,2,1:T(2,128)(2,1)}, bf16[2,4,10,10,512]{4,0,3,2,1:T(2,128)(2,1)})) %all-reduce.43.cloned.1.call-update) | async-done | bytes 1220624
  1011.1 40.0 %all-reduce.25 = (f32[512]{0:T(512)S(1)}, f32[512]{0:T(512)S(1)}) all-reduce(f32[512]{0:T(512)S(1)} %add.805, f32[512]{0:T(512)S(1)} %add.803), channel_id=1, replica_groups=mesh['batch'=8,'tm'=4] {'batch','tm'}, use_global_device_ids=true, to_apply=%region_48.49 | all-reduce | flops 1024 | bytes 8192 | tf_op jit(solution)/shard_map/psum | solution.py:164
  1089.7 38.8 %all-reduce.24 = (f32[1152]{0:T(1024)S(1)}, f32[1152]{0:T(1024)S(1)}) all-reduce(f32[1152]{0:T(1024)S(1)} %add_dynamic-update-slice_fusion, f32[1152]{0:T(1024)S(1)} %add_dynamic-update-slice_fusion.1), channel_id=1, replica_groups=mesh['batch'=8,'tm'=4] {'batch','tm'}, use_global_device_ids=true, to_apply=%region_54.55 | all-reduce | flops 2304 | bytes 18432 | tf_op jit(solution)/shard_map/psum | solution.py:164
  1222.1 13.1 fusion.6
  1242.7 19.0 %scatter-add.226 = f32[2,4,12,12,512]{4,3,2,1,0:T(8,128)S(1)} dynamic-update-slice(f32[2,4,12,12,512]{4,3,2,1,0:T(8,128)S(1)} %scatter-add.225, f32[2,4,10,10,512]{4,3,2,1,0:T(8,128)} %fusion.26, s32[]{:T(128)} %constant.1137.clone.1, s32[]{:T(128)} %constant.1137.clone.1, s32[]{:T(128)} %bitcast.134, s32[]{:T(128)} %bitcast.135, s32[]{:T(128)} %constant.1137.clone.1) | dynamic-update-slice | bytes 3276804 | tf_op jit(solution)/shard_map/scatter-add | solution.py:59
  1267.6 19.1 %scatter-add.229 = f32[2,4,12,12,512]{4,3,2,1,0:T(8,128)S(1)} dynamic-update-slice(f32[2,4,12,12,512]{4,3,2,1,0:T(8,128)S(1)} %scatter-add.226, f32[2,4,10,10,512]{4,3,2,1,0:T(8,128)} %add_select_fusion, s32[]{:T(128)} %constant.1137.clone.1, s32[]{:T(128)} %constant.1137.clone.1, s32[]{:T(128)} %bitcast.137, s32[]{:T(128)} %bitcast.138, s32[]{:T(128)} %constant.1137.clone.1) | dynamic-update-slice | bytes 3276804 | tf_op jit(solution)/shard_map/scatter-add | solution.py:59
  1290.5 17.8 %scatter-add.230 = f32[2,4,12,12,512]{4,3,2,1,0:T(8,128)S(1)} dynamic-update-slice(f32[2,4,12,12,512]{4,3,2,1,0:T(8,128)S(1)} %scatter-add.229, f32[2,4,10,10,512]{4,3,2,1,0:T(8,128)} %fusion.25, s32[]{:T(128)} %constant.1137.clone.1, s32[]{:T(128)} %constant.1137.clone.1, s32[]{:T(128)} %constant.1146.clone.1, s32[]{:T(128)} %constant.1137.clone.1, s32[]{:T(128)} %constant.1137.clone.1) | dynamic-update-slice | bytes 3276804 | tf_op jit(solution)/shard_map/scatter-add | solution.py:59
  1312.4 17.6 %scatter-add.231 = f32[2,4,12,12,512]{4,3,2,1,0:T(8,128)S(1)} dynamic-update-slice(f32[2,4,12,12,512]{4,3,2,1,0:T(8,128)S(1)} %scatter-add.230, f32[2,4,10,10,512]{4,3,2,1,0:T(8,128)} %fusion.24, s32[]{:T(128)} %constant.1137.clone.1, s32[]{:T(128)} %constant.1137.clone.1, s32[]{:T(128)} %constant.1146.clone.1, s32[]{:T(128)} %constant.1146.clone.1, s32[]{:T(128)} %constant.1137.clone.1) | dynamic-update-slice | bytes 3276804 | tf_op jit(solution)/shard_map/scatter-add | solution.py:59
  1334.1 17.6 %scatter-add.234 = f32[2,4,12,12,512]{4,3,2,1,0:T(8,128)S(1)} dynamic-update-slice(f32[2,4,12,12,512]{4,3,2,1,0:T(8,128)S(1)} %scatter-add.231, f32[2,4,10,10,512]{4,3,2,1,0:T(8,128)} %fusion.23, s32[]{:T(128)} %constant.1137.clone.1, s32[]{:T(128)} %constant.1137.clone.1, s32[]{:T(128)} %constant.1146.clone.1, s32[]{:T(128)} %constant.1147.clone.1, s32[]{:T(128)} %constant.1137.clone.1) | dynamic-update-slice | bytes 3276804 | tf_op jit(solution)/shard_map/scatter-add | solution.py:59
  1355.6 17.5 %scatter-add.235 = f32[2,4,12,12,512]{4,3,2,1,0:T(8,128)S(1)} dynamic-update-slice(f32[2,4,12,12,512]{4,3,2,1,0:T(8,128)S(1)} %scatter-add.234, f32[2,4,10,10,512]{4,3,2,1,0:T(8,128)} %fusion.22, s32[]{:T(128)} %constant.1137.clone.1, s32[]{:T(128)} %constant.1137.clone.1, s32[]{:T(128)} %constant.1147.clone.1, s32[]{:T(128)} %constant.1137.clone.1, s32[]{:T(128)} %constant.1137.clone.1) | dynamic-update-slice | bytes 3276804 | tf_op jit(solution)/shard_map/scatter-add | solution.py:59
  1377.2 17.5 %scatter-add.236 = f32[2,4,12,12,512]{4,3,2,1,0:T(8,128)S(1)} dynamic-update-slice(f32[2,4,12,12,512]{4,3,2,1,0:T(8,128)S(1)} %scatter-add.235, f32[2,4,10,10,512]{4,3,2,1,0:T(8,128)} %fusion.21, s32[]{:T(128)} %constant.1137.clone.1, s32[]{:T(128)} %constant.1137.clone.1, s32[]{:T(128)} %constant.1147.clone.1, s32[]{:T(128)} %constant.1146.clone.1, s32[]{:T(128)} %constant.1137.clone.1) | dynamic-update-slice | bytes 3276804 | tf_op jit(solution)/shard_map/scatter-add | solution.py:59
  1398.7 17.5 %scatter-add.239 = f32[2,4,12,12,512]{4,3,2,1,0:T(8,128)S(1)} dynamic-update-slice(f32[2,4,12,12,512]{4,3,2,1,0:T(8,128)S(1)} %scatter-add.236, f32[2,4,10,10,512]{4,3,2,1,0:T(8,128)} %fusion.20, s32[]{:T(128)} %constant.1137.clone.1, s32[]{:T(128)} %constant.1137.clone.1, s32[]{:T(128)} %constant.1147.clone.1, s32[]{:T(128)} %constant.1147.clone.1, s32[]{:T(128)} %constant.1137.clone.1) | dynamic-update-slice | bytes 3276804 | tf_op jit(solution)/shard_map/scatter-add | solution.py:59
  1421.0 37.6 %all-reduce.41.cloned.1.call-done = (bf16[2,4,7,7,512]{4,0,3,2,1:T(2,128)(2,1)}, bf16[2,4,10,10,512]{4,0,3,2,1:T(2,128)(2,1)}) async-done(((bf16[2,4,7,7,512]{4,0,3,2,1:T(2,128)(2,1)}, bf16[2,4,10,10,512]{4,0,3,2,1:T(2,128)(2,1)}), (bf16[2,4,7,7,512]{4,0,3,2,1:T(2,128)(2,1)}, bf16[2,4,10,10,512]{4,0,3,2,1:T(2,128)(2,1)})) %all-reduce.41.cloned.1.call-update) | async-done | bytes 1220624
  (560 shorter events, 699.1 us)
Async XLA Ops:
  18.2 9.1 all-to-all-start
  22.5 95.3 %all-gather.3.cloned.1.call-start = ((), (), s32[]{:S(2)}) async-start(), calls=%async_computation.9 | async-start | bytes 3981312 | tf_op jit(solution)/shard_map/all_gather | solution.py:204
  39.6 39.5 %all-to-all-start.1 = ((bf16[4,2,6912]{2,1,0:T(2,128)(2,1)}), bf16[4,2,6912]{2,1,0:T(2,128)(2,1)S(1)}, u32[]{:S(2)}, u32[]{:S(2)}) async-start(bf16[4,2,6912]{2,1,0:T(2,128)(2,1)} %reshape.2394), calls=%async_computation.1 | async-start | bytes 221184 | tf_op jit(solution)/shard_map/all_to_all | solution.py:199
  44.8 230.1 %all-reduce.47.cloned.1.call-start = ((), (), s32[]{:S(2)}) async-start(), calls=%async_computation.14 | async-start | bytes 2441216
  45.0 139.6 %copy-start.62 = (f32[288]{0:T(512)}, f32[288]{0:T(512)S(1)}, u32[]{:S(2)}) copy-start(f32[288]{0:T(512)S(1)} %get-tuple-element.753) | copy-start | bytes 3460
  45.0 139.6 %copy-start.66 = (f32[288]{0:T(512)}, f32[288]{0:T(512)S(1)}, u32[]{:S(2)}) copy-start(f32[288]{0:T(512)S(1)} %get-tuple-element.754) | copy-start | bytes 3460
  125.5 51.9 %copy-start.24 = (f32[2,4,7,7,288]{4,3,2,1,0:T(8,128)}, f32[2,4,7,7,288]{4,3,2,1,0:T(8,128)S(1)}, u32[]{:S(2)}) copy-start(f32[2,4,7,7,288]{4,3,2,1,0:T(8,128)S(1)} %get-tuple-element.749) | copy-start | bytes 1354756
  134.9 49.7 %copy-start.4 = (f32[2,4,10,10,288,1]{4,3,5,2,1,0:T(8,128)}, f32[2,4,10,10,288,1]{4,3,5,2,1,0:T(8,128)S(1)}, u32[]{:S(2)}) copy-start(f32[2,4,10,10,288,1]{4,3,5,2,1,0:T(8,128)S(1)} %get-tuple-element.750) | copy-start | bytes 2764804
  199.3 150.2 %all-gather.5.cloned.1.call-start = ((), (), s32[]{:S(2)}) async-start(), calls=%async_computation.10 | async-start | bytes 3981312 | tf_op jit(solution)/shard_map/all_gather | solution.py:206
  234.2 7.0 all-to-all-start.3
  238.6 304.7 %all-reduce.45.cloned.1.call-start = ((), (), s32[]{:S(2)}) async-start(), calls=%async_computation.13 | async-start | bytes 2441216
  238.7 97.0 %copy-start.64 = (f32[1,512]{1,0:T(1,128)}, f32[1,512]{1,0:T(1,128)S(1)}, u32[]{:S(2)}) copy-start(f32[1,512]{1,0:T(1,128)S(1)} %get-tuple-element.740) | copy-start | bytes 6148
  238.7 97.0 %copy-start.68 = (f32[1,512]{1,0:T(1,128)}, f32[1,512]{1,0:T(1,128)S(1)}, u32[]{:S(2)}) copy-start(f32[1,512]{1,0:T(1,128)S(1)} %get-tuple-element.741) | copy-start | bytes 6148
  276.5 58.7 %copy-start.37 = (bf16[2,1,7,7,512]{4,0,3,2,1:T(2,128)(2,1)}, bf16[2,1,7,7,512]{4,0,3,2,1:T(2,128)(2,1)S(1)}, u32[]{:S(2)}) copy-start(bf16[2,1,7,7,512]{4,0,3,2,1:T(2,128)(2,1)S(1)} %constant_dynamic-slice_fusion.11) | copy-start | bytes 301060
  278.2 57.5 %copy-start.29 = (bf16[2,1,10,10,512]{4,0,3,2,1:T(2,128)(2,1)}, bf16[2,1,10,10,512]{4,0,3,2,1:T(2,128)(2,1)S(1)}, u32[]{:S(2)}) copy-start(bf16[2,1,10,10,512]{4,0,3,2,1:T(2,128)(2,1)S(1)} %constant_dynamic-slice_fusion.10) | copy-start | bytes 614404
  356.5 50.2 %copy-start.10 = (f32[2,4,7,7,288,1]{4,3,0,2,1,5:T(8,128)}, f32[2,4,7,7,288,1]{4,3,0,2,1,5:T(8,128)S(1)}, u32[]{:S(2)}) copy-start(f32[2,4,7,7,288,1]{4,3,0,2,1,5:T(8,128)S(1)} %fusion.4) | copy-start | bytes 1354756
  434.0 573.1 %all-reduce.43.cloned.1.call-start = ((), (), s32[]{:S(2)}) async-start(), calls=%async_computation.12 | async-start | bytes 2441216
  538.6 49.7 %copy-start.49 = (bf16[2,1,7,7,512]{4,0,3,2,1:T(2,128)(2,1)S(1)}, bf16[2,1,7,7,512]{4,0,3,2,1:T(2,128)(2,1)}, u32[]{:S(2)}) copy-start(bf16[2,1,7,7,512]{4,0,3,2,1:T(2,128)(2,1)} %param.108) | copy-start | bytes 301060
  538.6 49.7 %copy-start.57 = (bf16[2,1,7,7,512]{4,0,3,2,1:T(2,128)(2,1)S(1)}, bf16[2,1,7,7,512]{4,0,3,2,1:T(2,128)(2,1)}, u32[]{:S(2)}) copy-start(bf16[2,1,7,7,512]{4,0,3,2,1:T(2,128)(2,1)} %param.118) | copy-start | bytes 301060
  538.6 50.5 %copy-start.46 = (bf16[2,1,10,10,512]{4,0,3,2,1:T(2,128)(2,1)S(1)}, bf16[2,1,10,10,512]{4,0,3,2,1:T(2,128)(2,1)}, u32[]{:S(2)}) copy-start(bf16[2,1,10,10,512]{4,0,3,2,1:T(2,128)(2,1)} %param.109) | copy-start | bytes 614404
  589.1 41.3 %copy-start.39 = (f32[2,1,7,7,512]{4,3,2,1,0:T(8,128)}, f32[2,1,7,7,512]{4,3,2,1,0:T(8,128)S(1)}, u32[]{:S(2)}) copy-start(f32[2,1,7,7,512]{4,3,2,1,0:T(8,128)S(1)} %get-tuple-element.710) | copy-start | bytes 602116
  591.3 49.0 %copy-start.27 = (f32[2,1,10,10,512]{4,3,2,1,0:T(8,128)}, f32[2,1,10,10,512]{4,3,2,1,0:T(8,128)S(1)}, u32[]{:S(2)}) copy-start(f32[2,1,10,10,512]{4,3,2,1,0:T(8,128)S(1)} %get-tuple-element.709) | copy-start | bytes 1228804
  981.4 29.3 %copy-start.30 = (bf16[2,1,10,10,512]{4,0,3,2,1:T(2,128)(2,1)S(1)}, bf16[2,1,10,10,512]{4,0,3,2,1:T(2,128)(2,1)}, u32[]{:S(2)}) copy-start(bf16[2,1,10,10,512]{4,0,3,2,1:T(2,128)(2,1)} %copy-done.29) | copy-start | bytes 614404
  981.4 69.7 %copy-start.73 = (f32[512]{0:T(512)S(1)}, f32[512]{0:T(512)}, u32[]{:S(2)}) copy-start(f32[512]{0:T(512)} %get-tuple-element.735) | copy-start | bytes 6148
  1086.6 42.1 %copy-start.70 = (f32[288]{0:T(512)S(1)}, f32[288]{0:T(512)}, u32[]{:S(2)}) copy-start(f32[288]{0:T(512)} %get-tuple-element.725) | copy-start | bytes 3460
  1161.7 300.4 %all-to-all-start.4 = ((bf16[8,24,64,288]{3,2,1,0:T(8,128)(2,1)}), bf16[8,24,64,288]{3,2,1,0:T(8,128)(2,1)}, u32[]{:S(2)}, u32[]{:S(2)}) async-start(bf16[8,24,64,288]{3,2,1,0:T(8,128)(2,1)} %copy.647), calls=%async_computation.4 | async-start | bytes 18874368 | tf_op jit(solution)/shard_map/all_to_all | solution.py:16
  1168.1 290.6 %all-reduce.41.cloned.1.call-start = ((), (), s32[]{:S(2)}) async-start(), calls=%async_computation.11 | async-start | bytes 2441216
  1416.7 45.2 %copy-start.28 = (f32[2,1,10,10,512]{4,3,2,1,0:T(8,128)S(1)}, f32[2,1,10,10,512]{4,3,2,1,0:T(8,128)}, u32[]{:S(2)}) copy-start(f32[2,1,10,10,512]{4,3,2,1,0:T(8,128)} %copy-done.27) | copy-start | bytes 1228804
  1468.6 8.3 all-to-all-start.8
  1476.9 9.0 all-to-all-start.6
  1485.9 10.1 all-to-all-start.7
  1496.0 10.2 all-to-all-start.5
  (70 other events, 517.7 us)
Sparse Core Ops, SparseCore 0:
  37.5 80.1 all-gather.2
  199.5 40.1 all-reduce.46
  242.7 74.8 all-gather.4
  434.1 39.3 all-reduce.44
  969.5 37.5 all-reduce.42
  1418.7 39.9 all-reduce.40
where the time goes:
time: 1540 us; the launch traced here: 1520 us
  local copies, waits for them, and re-layouts  646 us (42%)
  blocking collectives  480 us (31%)
  other arithmetic  149 us (10%)
  matrix products  111 us (7%)
  waiting for transfers between devices  72.4 us (5%)
  starting transfers between devices  41.7 us (3%)
  between operations  17 us (1%)
    scatter-add x36, local copies, waits for them, and re-layouts, space_spread(): padded.at[:, :, i:i + height, j:j + width]  342 us
    psum x4, blocking collectives, moments(): totals, squares = lax.psum((totals, squares), ('batch', 'tm'))  170 us
    psum x4, blocking collectives, norm_back(): gain_full, shift_full = lax.psum((gain_local, shift_local), ('batch', 'tm'))  158 us
    unnamed x245, local copies, waits for them, and re-layouts  143 us
    add x28, other arithmetic, space_spread(): padded.at[:, :, i:i + height, j:j + width]  79.7 us
    unnamed x10, waiting for transfers between devices  60.5 us
    all_gather x4, blocking collectives, whole_frames(): lax.all_gather(parts[1], 'tm', axis=1, tiled=True)  46.6 us
    dot_general x8, matrix products, contract_cols(): lax.dot_general(left, right, (((1,), (1,)), ((), ())), preferred_element_...  40.3 us
  transfers between devices with their start and end apart: 14, of which 8 were waited for; matrix products, arithmetic and copies ran while one was open for 29% of the time, Pallas kernels for 0%

commit v1 on v0

v1 whole, which is shorter than its diff:
```python
import jax
import jax.numpy as jnp
from jax import lax
from jax.sharding import PartitionSpec as P

EPS = 1e-05
F32 = jnp.float32
BF16 = jnp.bfloat16


def swap(value, axis, bit):
    n = lax.axis_size(axis)
    return lax.ppermute(value, axis, [(i, i ^ bit) for i in range(n)])


def batch_sum(value):
    n = lax.axis_size("batch")
    copies = jnp.broadcast_to(value[None], (n,) + value.shape)
    return jnp.sum(lax.all_to_all(copies, "batch", 0, 0, tiled=True), axis=0)


def tm_bits():
    t = lax.axis_index("tm")
    return t % 2, t // 2


def pair(first, second, bit):
    return jnp.where(bit == 0, jnp.stack([first, second]), jnp.stack([second, first]))


def halves(value, bit):
    h = value.shape[0] // 2
    mine = lax.dynamic_slice_in_dim(value, bit * h, h, 0)
    other = lax.dynamic_slice_in_dim(value, (1 - bit) * h, h, 0)
    return mine, other


def gather_tm(value):
    core, y = tm_bits()
    both = pair(value, swap(value, "tm", 2), y)
    all4 = pair(both, swap(both, "tm", 1), core)
    return jnp.swapaxes(all4, 0, 1).reshape((4,) + value.shape)


def sum_tm(value):
    core, y = tm_bits()
    mine, other = halves(value, core)
    mine = (mine + swap(other.astype(BF16), "tm", 1).astype(F32)).astype(BF16)
    mine = (mine.astype(F32) + swap(mine, "tm", 2).astype(F32)).astype(BF16)
    return pair(mine, swap(mine, "tm", 1), core).reshape(value.shape)


def scatter_tm(value):
    core, y = tm_bits()
    v = value.reshape((2, 2) + value.shape[1:])
    v = jnp.swapaxes(v, 0, 1)
    mine = lax.dynamic_index_in_dim(v, core, 0, keepdims=False)
    other = lax.dynamic_index_in_dim(v, 1 - core, 0, keepdims=False)
    mine = mine + swap(other.astype(BF16), "tm", 1).astype(F32)
    own = lax.dynamic_index_in_dim(mine, y, 0, keepdims=False)
    away = lax.dynamic_index_in_dim(mine, 1 - y, 0, keepdims=False)
    return own + swap(away.astype(BF16), "tm", 2).astype(F32)


DN = ("HWNC", "HWIO", "HWNC")


def conv(x, k):
    return lax.conv_general_dilated(
        x, k, (1, 1), "SAME", dimension_numbers=DN, preferred_element_type=F32
    )


def conv_weight_grad(x, g):
    return lax.conv_general_dilated(
        x, g, (1, 1), ((1, 1), (1, 1)), dimension_numbers=("HWNC"[:2] + "CN", "HWIO", "HWNC"),
        preferred_element_type=F32,
    )


class Shapes:
    def __init__(self, small, large):
        self.hs, self.hl = small, large
        self.ns, self.nl = small * small, large * large

    def split(self, rows):
        c = rows.shape[-1]
        n = rows.shape[0] // (self.ns + self.nl)
        cut = self.ns * n
        return (
            rows[:cut].reshape(self.hs, self.hs, n, c),
            rows[cut:].reshape(self.hl, self.hl, n, c),
        )

    @staticmethod
    def join(parts):
        return jnp.concatenate([p.reshape(-1, p.shape[-1]) for p in parts])


def conv_forward(shapes, rows, kernel):
    return shapes.join([conv(p, kernel) for p in shapes.split(rows)])


def conv_backward_input(shapes, rows, kernel):
    flipped = jnp.swapaxes(jnp.flip(kernel, (0, 1)), 2, 3)
    return shapes.join([conv(p, flipped) for p in shapes.split(rows)])


def conv_backward_kernel(shapes, rows, grads):
    out = 0.0
    for x, g in zip(shapes.split(rows), shapes.split(grads)):
        out = out + lax.conv_general_dilated(
            x, g, (1, 1), ((1, 1), (1, 1)), dimension_numbers=("HWCN", "HWIO", "HWNC"),
            preferred_element_type=F32,
        )
    return out


def frames_shifted(rows, frames, by):
    c = rows.shape[-1]
    v = rows.reshape(-1, frames, c)
    if by == 1:
        v = jnp.concatenate([v[:, 1:], jnp.zeros_like(v[:, :1])], axis=1)
    elif by == -1:
        v = jnp.concatenate([jnp.zeros_like(v[:, :1]), v[:, :-1]], axis=1)
    return v.reshape(-1, c)


def sums(a, b):
    return jnp.stack([jnp.sum(a, axis=0), jnp.sum(b, axis=0)])


def stats_of(rows, counted):
    s = batch_sum(sums(rows, rows * rows)) / counted
    mean = s[0]
    return mean, lax.rsqrt(s[1] - mean * mean + EPS)


def slope(v):
    sig = jax.nn.sigmoid(v)
    return sig * (1.0 + v * (1.0 - sig))


def norm_back(e, xhat, gain, inverse, counted):
    s = batch_sum(sums(e * xhat, e))
    dgain, dshift = s[0], s[1]
    dv = gain * inverse * (e - (dshift + xhat * dgain) / counted)
    return dv, dgain, dshift


def fetch_kernels(spatial, temporal):
    both = jnp.concatenate([spatial, jnp.swapaxes(temporal, 1, 2)], axis=0)
    n = lax.axis_size("tm")
    k, r, m = both.shape
    moved = lax.all_to_all(both, "tm", split_axis=2, concat_axis=1, tiled=True)
    whole = lax.all_gather(moved, "batch", axis=0)
    whole = jnp.swapaxes(whole, 0, 1).reshape(k, -1, m // n)
    return whole[:9], whole[9:]


def return_kernels(grad_s, grad_t):
    both = jnp.concatenate([grad_s, grad_t], axis=0).astype(BF16)
    k, c, m = both.shape
    nb, nt = lax.axis_size("batch"), lax.axis_size("tm")
    own = c // (nb * nt)
    pieces = jnp.swapaxes(both.reshape(k, nb * nt, own, m), 0, 1)
    moved = lax.all_to_all(pieces, ("batch", "tm"), 0, 0, tiled=True)
    moved = moved.reshape(nb, nt, k, own, m)
    summed = jnp.sum(moved.astype(F32), axis=0)
    summed = jnp.moveaxis(summed, 0, 2).reshape(k, own, nt * m)
    return summed[:9], jnp.swapaxes(summed[9:], 1, 2)


def body(
    input_small, input_large, spatial_one, temporal_one, spatial_two, temporal_two,
    mid_gain, mid_shift, out_gain, out_shift, cotangent_small, cotangent_large,
):
    clips = input_small.shape[0]
    frames = lax.axis_size("tm")
    shapes = Shapes(input_small.shape[2], input_large.shape[2])
    places = shapes.ns + shapes.nl
    counted = float(places * clips * frames * lax.axis_size("batch"))
    t = lax.axis_index("tm")

    def to_rows(small, large):
        out = []
        for v in (small, large):
            v = v[:, 0].reshape(clips, -1, v.shape[-1])
            out.append(jnp.swapaxes(v, 0, 1).reshape(-1, v.shape[-1]))
        return jnp.concatenate(out)

    def from_rows(rows):
        v = jnp.swapaxes(rows.reshape(places, clips, -1), 0, 1)
        s = v[:, : shapes.ns].reshape(clips, 1, shapes.hs, shapes.hs, -1)
        l = v[:, shapes.ns :].reshape(clips, 1, shapes.hl, shapes.hl, -1)
        return s, l

    def whole_rows(rows):
        g = gather_tm(rows)
        return jnp.moveaxis(g, 0, 1).reshape(-1, rows.shape[-1])

    def frame_pieces(rows):
        return jnp.moveaxis(rows.reshape(-1, frames, rows.shape[-1]), 1, 0)

    k_sa, k_ta = fetch_kernels(spatial_one, temporal_one)
    k_sb, k_tb = fetch_kernels(spatial_two, temporal_two)
    mid = k_sa.shape[2]
    chans = k_sa.shape[1]
    k_sa = k_sa.reshape(3, 3, chans, mid)
    k_sb = k_sb.reshape(3, 3, chans, mid)

    def mine(v):
        return lax.dynamic_slice_in_dim(v, t * mid, mid, 0)

    x = whole_rows(to_rows(input_small, input_large))
    cot = whole_rows(to_rows(cotangent_small, cotangent_large))

    def temporal(a, k):
        y = lax.dot_general(a, k.reshape(3 * chans, mid), (((1,), (1,)), ((), ())), preferred_element_type=F32)
        return (
            frames_shifted(y[:, :chans], frames, -1)
            + y[:, chans : 2 * chans]
            + frames_shifted(y[:, 2 * chans :], frames, 1)
        )

    def temporal_back(a, g, k):
        wide = jnp.concatenate(
            [frames_shifted(g, frames, 1), g, frames_shifted(g, frames, -1)], axis=1
        )
        da = lax.dot_general(wide, k.reshape(3 * chans, mid), (((1,), (0,)), ((), ())), preferred_element_type=F32)
        dk = lax.dot_general(wide, a, (((0,), (0,)), ((), ())), preferred_element_type=F32)
        return da.astype(BF16), dk.reshape(3, chans, mid)

    def forward_half(x, ks, kt, gm, sm, go, so):
        s1 = conv_forward(shapes, x, ks)
        m1, r1 = stats_of(s1, counted)
        xh1 = (s1 - m1) * r1
        p1 = gm * xh1 + sm
        a1 = jax.nn.silu(p1).astype(BF16)
        t1 = sum_tm(temporal(a1, kt)).astype(F32)
        m2, r2 = stats_of(t1, counted)
        xh2 = (t1 - m2) * r2
        p2 = go * xh2 + so
        return (xh1, p1, r1, a1), (xh2, p2, r2)

    gm0, gm1, sm0, sm1 = mine(mid_gain[0]), mine(mid_gain[1]), mine(mid_shift[0]), mine(mid_shift[1])
    (xh1, p1, r1, a1), (xh2, p2, r2) = forward_half(x, k_sa, k_ta, gm0, sm0, out_gain[0], out_shift[0])
    b1 = jax.nn.silu(p2).astype(BF16)
    (xh3, p3, r3, a2), (xh4, p4, r4) = forward_half(b1, k_sb, k_tb, gm1, sm1, out_gain[1], out_shift[1])
    pre = x.astype(F32) + p4
    dpre = cot.astype(F32) * slope(pre)
    own_pre = lax.dynamic_index_in_dim(frame_pieces(pre), t, 0, keepdims=False)
    own_dpre = lax.dynamic_index_in_dim(frame_pieces(dpre), t, 0, keepdims=False)
    out_s, out_l = from_rows(jax.nn.silu(own_pre).astype(BF16))

    dt2, dg4, ds4 = norm_back(dpre, xh4, out_gain[1], r4, counted)
    da2, dk_tb = temporal_back(a2, dt2.astype(BF16), k_tb)
    e3 = da2.astype(F32) * slope(p3)
    ds2, dg3, ds3 = norm_back(e3, xh3, gm1, r3, counted)
    ds2 = ds2.astype(BF16)
    dk_sb = conv_backward_kernel(shapes, b1, ds2).reshape(9, chans, mid)
    grad_sb, grad_tb = return_kernels(dk_sb, dk_tb)
    db1 = sum_tm(conv_backward_input(shapes, ds2, k_sb)).astype(F32)
    e2 = db1 * slope(p2)
    dt1, dg2, ds2_ = norm_back(e2, xh2, out_gain[0], r2, counted)
    da1, dk_ta = temporal_back(a1, dt1.astype(BF16), k_ta)
    e1 = da1.astype(F32) * slope(p1)
    ds1, dg1, ds1_ = norm_back(e1, xh1, gm0, r1, counted)
    ds1 = ds1.astype(BF16)
    dk_sa = conv_backward_kernel(shapes, x, ds1).reshape(9, chans, mid)
    grad_sa, grad_ta = return_kernels(dk_sa, dk_ta)
    din = scatter_tm(frame_pieces(conv_backward_input(shapes, ds1, k_sa)))
    grad_s, grad_l = from_rows(own_dpre + din)

    mids = lax.all_gather(jnp.stack([dg1, dg3, ds1_, ds3]), "tm", axis=1, tiled=True)
    return (
        out_s, out_l, grad_s, grad_l, grad_sa, grad_ta, grad_sb, grad_tb,
        mids[:2], mids[2:], jnp.stack([dg2, dg4]), jnp.stack([ds2_, ds4]),
    )


def solution(mesh):
    act = P("batch", "tm", None, None, None)
    rows = P(None, ("batch", "tm"), None)
    cols = P(None, None, ("batch", "tm"))
    return jax.shard_map(
        body,
        mesh=mesh,
        in_specs=(act, act, rows, cols, rows, cols, P(), P(), P(), P(), act, act),
        out_specs=(act, act, act, act, rows, cols, rows, cols, P(), P(), P(), P()),
        check_vma=False,
    )
```

time: 1540 us -> 767 us (0.50)
  blocking collectives: 480 us -> 25 us
  local copies, waits for them, and re-layouts: 646 us -> 237 us
  waiting for transfers between devices: 72.4 us -> 229 us
  other arithmetic: 149 us -> 98.8 us
  matrix products: 111 us -> 69.4 us
  starting transfers between devices: 41.7 us -> 78.3 us
    scatter-add x40 -> x0, local copies, waits for them, and re-layouts: 342 us -> none  [the longest x36 342 us: space_spread(): padded.at[:, :, i:i + height, j:j + width]]
    psum x8 -> x0, blocking collectives: 328 us -> none  [the longest x4 170 us: moments(): totals, squares = lax.psum((totals, squares), ('batch', 'tm'))]
    all_gather x10 -> x1, blocking collectives: 141 us -> 6.14 us  [body(): lax.all_gather(jnp.stack([dg1, dg3, ds1_, ds3]), 'tm', axis=1, tiled=True)]
    all_to_all x8 -> x10, waiting for transfers between devices: 11 us -> 139 us  [the longest x2 131 us: return_kernels(): moved = lax.all_to_all(pieces, ('batch', 'tm'), 0, 0, tiled=True)]
    unnamed x245 -> x181, local copies, waits for them, and re-layouts: 143 us -> 38.3 us
    dot_general x24 -> x6, matrix products: 111 us -> 23.8 us  [the longest x2 8.63 us: temporal_back(): lax.dot_general(wide, k.reshape(3 * chans, mid), (((1,), (0,)), ((), ()))...]
    add x38 -> x4, other arithmetic: 79.9 us -> 8.77 us  [the longest x2 7.35 us: temporal(): frames_shifted(y[:, :chans], frames, -1) + y[:, chans:2 * chans]]
    ppermute x0 -> x15, waiting for transfers between devices: none -> 60.8 us  [swap(): return lax.ppermute(value, axis, [(i, i ^ bit) for i in range(n)])]
  transfers between devices with their start and end apart: 14 -> 27, of which waited for: 8 -> 15; matrix products, arithmetic and copies ran while one was open for 29% -> 28% of each run, Pallas kernels for 0% -> 0%
where the time goes in v1:
time: 767 us; the launch traced here: 753 us
  local copies, waits for them, and re-layouts  237 us (31%)
  waiting for transfers between devices  229 us (30%)
  other arithmetic  98.8 us (13%)
  starting transfers between devices  78.3 us (10%)
  matrix products  69.4 us (9%)
  blocking collectives  25 us (3%)
  between operations  15.9 us (2%)
    all_to_all x2, waiting for transfers between devices, return_kernels(): moved = lax.all_to_all(pieces, ('batch', 'tm'), 0, 0, tiled=True)  131 us
    ppermute x15, waiting for transfers between devices, swap(): return lax.ppermute(value, axis, [(i, i ^ bit) for i in range(n)])  60.8 us
    unnamed x181, local copies, waits for them, and re-layouts  38.3 us
    all_to_all x7, starting transfers between devices, batch_sum(): return jnp.sum(lax.all_to_all(copies, 'batch', 0, 0, tiled=True), axis=0)  37.8 us
    conv_general_dilated x8, matrix products, conv(): lax.conv_general_dilated(x, k, (1, 1), 'SAME', dimension_numbers=DN, pref...  32.9 us
    all_gather x2, waiting for transfers between devices, fetch_kernels(): whole = lax.all_gather(moved, 'batch', axis=0)  29.3 us
    reshape x8, local copies, waits for them, and re-layouts, frames_shifted(): return v.reshape(-1, c)  24.9 us
    ppermute x15, starting transfers between devices, swap(): return lax.ppermute(value, axis, [(i, i ^ bit) for i in range(n)])  20.1 us
  transfers between devices with their start and end apart: 27, of which 15 were waited for; matrix products, arithmetic and copies ran while one was open for 28% of the time, Pallas kernels for 0%

profile of v1, /device:TPU:13, one launch (start us, length us, event | category | flops | bytes accessed | tf_op | source)
XLA Modules:
  0.0 752.8 jit_solution(6390409764154274004)
XLA Ops:
  8.3 5.2 copy.341
  13.5 5.5 reshape.710
  19.0 9.3 %all_to_all.80 = bf16[4,2,27648]{2,1,0:T(2,128)(2,1)S(1)} all-to-all(bf16[4,2,27648]{2,1,0:T(2,128)(2,1)S(1)} %reshape.710), channel_id=1, replica_groups=mesh['batch'=8,'tm'=4] {'tm'}, dimensions={0} | all-to-all | bytes 884736 | tf_op jit(solution)/shard_map/all_to_all | solution.py:155
  28.3 5.5 reshape.711
  33.8 6.7 copy.398
  43.2 6.7 collective-permute-done
  52.4 5.2 copy.351
  57.6 6.2 reshape.708
  69.6 5.2 all-to-all-done.3
  74.8 5.5 reshape.709
  80.3 6.7 copy.399
  92.0 28.8 %all-gather.4.cloned.1.call-done = bf16[8,12,64,288]{3,2,1,0:T(8,128)(2,1)} async-done(((bf16[1,12,64,288]{3,2,1,0:T(8,128)(2,1)}), bf16[8,12,64,288]{3,2,1,0:T(8,128)(2,1)}) %all-gather.4.cloned.1.call-update) | async-done | bytes 3538960 | tf_op jit(solution)/shard_map/all_gather | solution.py:156
  139.9 5.2 all-to-all-start.1
  184.1 14.9 %collective-permute-done.3 = bf16[596,512]{1,0:T(8,128)(2,1)S(1)} collective-permute-done((bf16[596,512]{1,0:T(8,128)(2,1)S(1)}, bf16[596,512]{1,0:T(8,128)(2,1)S(1)}, u32[]{:S(2)}, u32[]{:S(2)}) %collective-permute-start.3) | collective-permute-done | bytes 610336 | tf_op jit(solution)/shard_map/ppermute | solution.py:13
  207.8 5.6 all-to-all-start.2
  225.8 5.6 fusion.63
  243.7 5.7 all-to-all-start.4
  305.9 16.1 %collective-permute-done.8 = bf16[298,512]{1,0:T(8,128)(2,1)S(1)} collective-permute-done((bf16[298,512]{1,0:T(8,128)(2,1)S(1)}, bf16[298,512]{1,0:T(8,128)(2,1)S(1)}, u32[]{:S(2)}, u32[]{:S(2)}) %collective-permute-start.8) | collective-permute-done | bytes 305184 | tf_op jit(solution)/shard_map/ppermute | solution.py:13
  329.1 5.6 all-to-all-start.5
  344.7 6.7 multiply_reduce_fusion
  352.1 5.5 all-to-all-start.6
  406.8 9.5 %all_to_all.81 = f32[8,2,288]{2,1,0:T(2,128)} all-to-all(f32[8,2,288]{2,1,0:T(2,128)S(1)} %broadcast_in_dim.21), channel_id=1, replica_groups=mesh['batch'=8,'tm'=4] {'batch'}, dimensions={0} | all-to-all | bytes 36864 | tf_op jit(solution)/shard_map/all_to_all | solution.py:19
  425.4 5.4 fusion.65
  449.8 10.0 %collective-permute-done.11 = bf16[596,512]{1,0:T(8,128)(2,1)} collective-permute-done((bf16[596,512]{1,0:T(8,128)(2,1)S(1)}, bf16[596,512]{1,0:T(8,128)(2,1)}, u32[]{:S(2)}, u32[]{:S(2)}) %collective-permute-start.11) | collective-permute-done | bytes 610336 | tf_op jit(solution)/shard_map/ppermute | solution.py:13
  502.7 5.8 multiply_reduce_fusion.4
  509.1 5.7 all-to-all-start.9
  520.0 6.3 all-to-all-start.11
  551.0 77.6 %all-to-all-done.11 = bf16[32,12,16,288]{3,2,1,0:T(8,128)(2,1)} async-done(((bf16[32,12,16,288]{3,2,1,0:T(8,128)(2,1)}), bf16[32,12,16,288]{3,2,1,0:T(8,128)(2,1)}, u32[]{:S(2)}, u32[]{:S(2)}) %all-to-all-start.11) | async-done | bytes 3538976 | tf_op jit(solution)/shard_map/all_to_all | solution.py:167
  628.6 9.0 %all-to-all-start.10 = ((bf16[32,12,16,288]{3,2,1,0:T(8,128)(2,1)}), bf16[32,12,16,288]{3,2,1,0:T(8,128)(2,1)}, u32[]{:S(2)}, u32[]{:S(2)}) async-start(bf16[32,12,16,288]{3,2,1,0:T(8,128)(2,1)} %copy.385), calls=%async_computation.10 | async-start | bytes 9437184 | tf_op jit(solution)/shard_map/all_to_all | solution.py:167
  657.9 6.1 all-gather
  666.7 9.6 %collective-permute-done.14 = bf16[298,512]{1,0:T(8,128)(2,1)S(1)} collective-permute-done((bf16[298,512]{1,0:T(8,128)(2,1)S(1)}, bf16[298,512]{1,0:T(8,128)(2,1)S(1)}, u32[]{:S(2)}, u32[]{:S(2)}) %collective-permute-start.14) | collective-permute-done | bytes 305184 | tf_op jit(solution)/shard_map/ppermute | solution.py:13
  686.1 53.6 %all-to-all-done.10 = bf16[32,12,16,288]{3,2,1,0:T(8,128)(2,1)} async-done(((bf16[32,12,16,288]{3,2,1,0:T(8,128)(2,1)}), bf16[32,12,16,288]{3,2,1,0:T(8,128)(2,1)}, u32[]{:S(2)}, u32[]{:S(2)}) %all-to-all-start.10) | async-done | bytes 3538976 | tf_op jit(solution)/shard_map/all_to_all | solution.py:167
  (439 shorter events, 370.9 us)
Async XLA Ops:
  7.2 113.7 %all-gather.4.cloned.1.call-start = ((), (), s32[]{:S(2)}) async-start(), calls=%async_computation.12 | async-start | bytes 5308416 | tf_op jit(solution)/shard_map/all_gather | solution.py:156
  41.7 8.2 %collective-permute-start = (bf16[298,512]{1,0:T(8,128)(2,1)S(1)}, bf16[298,512]{1,0:T(8,128)(2,1)S(1)}, u32[]{:S(2)}, u32[]{:S(2)}) collective-permute-start(bf16[298,512]{1,0:T(8,128)(2,1)S(1)} %get-tuple-element.149), channel_id=1, source_target_pairs={{0,2},{1,3},{2,0},{3,1},{4,6},{5,7},{6,4},{7,5},{8,10},{9,11},{10,... | collective-permute-start | bytes 915464 | tf_op jit(solution)/shard_map/ppermute | solution.py:13
  50.7 37.3 %collective-permute-start.1 = (bf16[2,298,512]{2,0,1:T(2,128)(2,1)S(1)}, bf16[2,298,512]{2,0,1:T(2,128)(2,1)S(1)}, u32[]{:S(2)}, u32[]{:S(2)}) collective-permute-start(bf16[2,298,512]{2,0,1:T(2,128)(2,1)S(1)} %copy.337), channel_id=1, source_target_pairs={{0,1},{1,0},{2,3},{3,2},{4,5},{5,4},{6,7},{7,6},{8,9},{9,8},{10,11... | collective-permute-start | bytes 1830920 | tf_op jit(solution)/shard_map/ppermute | solution.py:13
  63.8 10.9 %all-to-all-start.3 = ((bf16[4,2,27648]{2,1,0:T(2,128)(2,1)}), bf16[4,2,27648]{2,1,0:T(2,128)(2,1)S(1)}, u32[]{:S(2)}, u32[]{:S(2)}) async-start(bf16[4,2,27648]{2,1,0:T(2,128)(2,1)} %reshape.708), calls=%async_computation.3 | async-start | bytes 884736 | tf_op jit(solution)/shard_map/all_to_all | solution.py:155
  68.7 133.5 %all-gather.6.cloned.1.call-start = ((), (), s32[]{:S(2)}) async-start(), calls=%async_computation.13 | async-start | bytes 5308416 | tf_op jit(solution)/shard_map/all_gather | solution.py:156
  137.3 12.7 %copy-start.23 = (f32[392,288]{0,1:T(8,128)}, f32[392,288]{0,1:T(8,128)S(1)}, u32[]{:S(2)}) copy-start(f32[392,288]{0,1:T(8,128)S(1)} %copy.346) | copy-start | bytes 1354756
  139.9 9.4 %all-to-all-start.1 = ((f32[8,2,288]{2,1,0:T(2,128)}), f32[8,2,288]{2,1,0:T(2,128)S(1)}, u32[]{:S(2)}, u32[]{:S(2)}) async-start(f32[8,2,288]{2,1,0:T(2,128)} %broadcast_in_dim.16), calls=%async_computation.1 | async-start | bytes 49152 | tf_op jit(solution)/shard_map/all_to_all | solution.py:19
  177.7 23.4 %copy-start.74 = (f32[2,512]{1,0:T(2,128)S(1)}, f32[2,512]{1,0:T(2,128)}, u32[]{:S(2)}) copy-start(f32[2,512]{1,0:T(2,128)} %param.21) | copy-start | bytes 12292
  177.7 4.6 collective-permute-start.2
  183.8 15.2 %collective-permute-start.3 = (bf16[596,512]{1,0:T(8,128)(2,1)S(1)}, bf16[596,512]{1,0:T(8,128)(2,1)S(1)}, u32[]{:S(2)}, u32[]{:S(2)}) collective-permute-start(bf16[596,512]{1,0:T(8,128)(2,1)S(1)} %add_convert_fusion.6), channel_id=1, source_target_pairs={{0,2},{1,3},{2,0},{3,1},{4,6},{5,7},{6,4},{7,5},{8,10},{9,11},{10,... | collective-permute-start | bytes 1830920 | tf_op jit(solution)/shard_map/ppermute | solution.py:13
  200.0 5.0 collective-permute-start.4
  207.8 12.5 %all-to-all-start.2 = ((f32[8,2,512]{2,1,0:T(2,128)}), f32[8,2,512]{2,1,0:T(2,128)}, u32[]{:S(2)}, u32[]{:S(2)}) async-start(f32[8,2,512]{2,1,0:T(2,128)} %broadcast_in_dim.17), calls=%async_computation.2 | async-start | bytes 65536 | tf_op jit(solution)/shard_map/all_to_all | solution.py:19
  243.7 9.9 %all-to-all-start.4 = ((f32[8,2,288]{2,1,0:T(2,128)}), f32[8,2,288]{2,1,0:T(2,128)}, u32[]{:S(2)}, u32[]{:S(2)}) async-start(f32[8,2,288]{2,1,0:T(2,128)} %broadcast_in_dim.18), calls=%async_computation.4 | async-start | bytes 49152 | tf_op jit(solution)/shard_map/all_to_all | solution.py:19
  293.8 5.1 collective-permute-start.5
  300.0 24.0 %collective-permute-start.6 = (bf16[596,512]{1,0:T(8,128)(2,1)}, bf16[596,512]{1,0:T(8,128)(2,1)}, u32[]{:S(2)}, u32[]{:S(2)}) collective-permute-start(bf16[596,512]{1,0:T(8,128)(2,1)} %add_convert_fusion.4), channel_id=1, source_target_pairs={{0,2},{1,3},{2,0},{3,1},{4,6},{5,7},{6,4},{7,5},{8,10},{9,11},{10,... | collective-permute-start | bytes 1830920 | tf_op jit(solution)/shard_map/ppermute | solution.py:13
  304.7 17.3 %collective-permute-start.8 = (bf16[298,512]{1,0:T(8,128)(2,1)S(1)}, bf16[298,512]{1,0:T(8,128)(2,1)S(1)}, u32[]{:S(2)}, u32[]{:S(2)}) collective-permute-start(bf16[298,512]{1,0:T(8,128)(2,1)S(1)} %get-tuple-element.146), channel_id=1, source_target_pairs={{0,2},{1,3},{2,0},{3,1},{4,6},{5,7},{6,4},{7,5},{8,10},{9,11},{10,... | collective-permute-start | bytes 915464 | tf_op jit(solution)/shard_map/ppermute | solution.py:13
  322.7 2.9 collective-permute-start.9
  325.4 2.2 collective-permute-start.7
  329.1 12.2 %all-to-all-start.5 = ((f32[8,2,512]{2,1,0:T(2,128)}), f32[8,2,512]{2,1,0:T(2,128)}, u32[]{:S(2)}, u32[]{:S(2)}) async-start(f32[8,2,512]{2,1,0:T(2,128)} %broadcast_in_dim.19), calls=%async_computation.5 | async-start | bytes 65536 | tf_op jit(solution)/shard_map/all_to_all | solution.py:19
  352.1 27.2 %all-to-all-start.6 = ((f32[8,2,512]{2,1,0:T(2,128)}), f32[8,2,512]{2,1,0:T(2,128)}, u32[]{:S(2)}, u32[]{:S(2)}) async-start(f32[8,2,512]{2,1,0:T(2,128)} %broadcast_in_dim.20), calls=%async_computation.6 | async-start | bytes 65536 | tf_op jit(solution)/shard_map/all_to_all | solution.py:19
  437.6 4.7 collective-permute-start.10
  444.4 15.4 %collective-permute-start.11 = (bf16[596,512]{1,0:T(8,128)(2,1)S(1)}, bf16[596,512]{1,0:T(8,128)(2,1)}, u32[]{:S(2)}, u32[]{:S(2)}) collective-permute-start(bf16[596,512]{1,0:T(8,128)(2,1)S(1)} %fusion.16), channel_id=1, source_target_pairs={{0,2},{1,3},{2,0},{3,1},{4,6},{5,7},{6,4},{7,5},{8,10},{9,11},{10,... | collective-permute-start | bytes 1830920 | tf_op jit(solution)/shard_map/ppermute | solution.py:13
  448.0 14.2 %copy-start.40 = (bf16[800,512]{1,0:T(8,128)(2,1)S(1)}, bf16[800,512]{1,0:T(8,128)(2,1)}, u32[]{:S(2)}) copy-start(bf16[800,512]{1,0:T(8,128)(2,1)} %copy-done.39) | copy-start | bytes 2457604
  461.1 10.4 %collective-permute-start.12 = (bf16[596,512]{1,0:T(8,128)(2,1)S(1)}, bf16[596,512]{1,0:T(8,128)(2,1)}, u32[]{:S(2)}, u32[]{:S(2)}) collective-permute-start(bf16[596,512]{1,0:T(8,128)(2,1)S(1)} %add_convert_fusion.2), channel_id=1, source_target_pairs={{0,1},{1,0},{2,3},{3,2},{4,5},{5,4},{6,7},{7,6},{8,9},{9,8},{10,11... | collective-permute-start | bytes 1830920 | tf_op jit(solution)/shard_map/ppermute | solution.py:13
  475.5 9.6 %all-to-all-start.8 = ((f32[8,2,512]{2,1,0:T(2,128)}), f32[8,2,512]{2,1,0:T(2,128)S(1)}, u32[]{:S(2)}, u32[]{:S(2)}) async-start(f32[8,2,512]{2,1,0:T(2,128)} %broadcast_in_dim.22), calls=%async_computation.8 | async-start | bytes 65536 | tf_op jit(solution)/shard_map/all_to_all | solution.py:19
  502.7 12.1 %copy-start.8 = (bf16[3,3,512,288]{3,2,1,0:T(8,128)(2,1)S(1)}, bf16[3,3,512,288]{3,2,1,0:T(8,128)(2,1)}, u32[]{:S(2)}) copy-start(bf16[3,3,512,288]{3,2,1,0:T(8,128)(2,1)} %copy.389) | copy-start | bytes 7962628
  509.1 10.8 %all-to-all-start.9 = ((f32[8,2,288]{2,1,0:T(2,128)}), f32[8,2,288]{2,1,0:T(2,128)}, u32[]{:S(2)}, u32[]{:S(2)}) async-start(f32[8,2,288]{2,1,0:T(2,128)} %broadcast_in_dim.23), calls=%async_computation.9 | async-start | bytes 49152 | tf_op jit(solution)/shard_map/all_to_all | solution.py:19
  520.0 108.6 %all-to-all-start.11 = ((bf16[32,12,16,288]{3,2,1,0:T(8,128)(2,1)}), bf16[32,12,16,288]{3,2,1,0:T(8,128)(2,1)}, u32[]{:S(2)}, u32[]{:S(2)}) async-start(bf16[32,12,16,288]{3,2,1,0:T(8,128)(2,1)} %copy.391), calls=%async_computation.11 | async-start | bytes 9437184 | tf_op jit(solution)/shard_map/all_to_all | solution.py:167
  628.6 13.3 %copy-start.1 = (bf16[9,8,64,288]{3,2,1,0:T(8,128)(2,1)S(1)}, bf16[9,8,64,288]{3,2,1,0:T(8,128)(2,1)}, u32[]{:S(2)}) copy-start(bf16[9,8,64,288]{3,2,1,0:T(8,128)(2,1)} %copy-done) | copy-start | bytes 7962628
  628.6 111.1 %all-to-all-start.10 = ((bf16[32,12,16,288]{3,2,1,0:T(8,128)(2,1)}), bf16[32,12,16,288]{3,2,1,0:T(8,128)(2,1)}, u32[]{:S(2)}, u32[]{:S(2)}) async-start(bf16[32,12,16,288]{3,2,1,0:T(8,128)(2,1)} %copy.385), calls=%async_computation.10 | async-start | bytes 9437184 | tf_op jit(solution)/shard_map/all_to_all | solution.py:167
  654.1 10.0 %collective-permute-start.13 = (bf16[2,298,512]{2,0,1:T(2,128)(2,1)}, bf16[2,298,512]{2,0,1:T(2,128)(2,1)S(1)}, u32[]{:S(2)}, u32[]{:S(2)}) collective-permute-start(bf16[2,298,512]{2,0,1:T(2,128)(2,1)} %copy.381), channel_id=1, source_target_pairs={{0,1},{1,0},{2,3},{3,2},{4,5},{5,4},{6,7},{7,6},{8,9},{9,8},{10,11... | collective-permute-start | bytes 1830920 | tf_op jit(solution)/shard_map/ppermute | solution.py:13
  664.4 11.9 %collective-permute-start.14 = (bf16[298,512]{1,0:T(8,128)(2,1)S(1)}, bf16[298,512]{1,0:T(8,128)(2,1)S(1)}, u32[]{:S(2)}, u32[]{:S(2)}) collective-permute-start(bf16[298,512]{1,0:T(8,128)(2,1)S(1)} %fusion.22), channel_id=1, source_target_pairs={{0,2},{1,3},{2,0},{3,1},{4,6},{5,7},{6,4},{7,5},{8,10},{9,11},{10,... | collective-permute-start | bytes 915464 | tf_op jit(solution)/shard_map/ppermute | solution.py:13
  (79 other events, 353.0 us)
Sparse Core Ops, SparseCore 0:
  41.6 79.2 all-gather.3
  123.6 78.4 all-gather.5
